TPU v7x, 512 devices: a whole 4x4x16 slice. The times are simulated.
512 devices in a mesh: grp: 16 (over y, x), tile: 32 (over z, core).
Axes of the slice: x: 4, y: 4, z: 16, core: 2. Of those that a mesh axis runs over, the one named last changes fastest.
Arguments:
- latent: bfloat16 [8, 64, 64, 512], P(None, 'grp', 'tile'), may hold values from -36 to 36
- coarse_filters: bfloat16 [3, 3, 3, 512, 512], P(None, None, None, None, 'grp'), may hold values from -0.0546875 to 0.0546875
- mid_filters: bfloat16 [3, 3, 3, 256, 256], P(None, None, None, None, 'tile'), may hold values from -0.078125 to 0.078125
- fine_filters: bfloat16 [3, 3, 3, 128, 128], replicated, may hold values from -0.109375 to 0.109375
- coarse_proj: bfloat16 [512, 256], replicated, may hold values from -0.25 to 0.25
- mid_proj: bfloat16 [256, 128], replicated, may hold values from -0.375 to 0.375
Outputs:
- frames_out: bfloat16 [8, 256, 256, 128], P(None, 'grp', 'tile')
All inputs are finite; a program needn't handle non-finite values.
Results may differ from a plain program's by a relative error of at most 0.018.
Values may be sent and summed in bfloat16 or wider, within the bound.
A program may use at most 128 MiB of HBM per device.

v0:
```python
import jax
import jax.numpy as jnp
from jax import lax
from jax.sharding import PartitionSpec as P


def with_halo(shard, sides, width):
    for axis, dim in sides:
        size, length = (lax.axis_size(axis), shard.shape[dim])
        up = [(i, (i + 1) % size) for i in range(size - 1)]
        down = [(j, i) for i, j in up]
        last = lax.slice_in_dim(shard, length - width, length, axis=dim)
        initial = lax.slice_in_dim(shard, 0, width, axis=dim)
        before = lax.ppermute(last, axis, up)
        after = lax.ppermute(initial, axis, down)
        shard = jnp.concatenate([before, shard, after], axis=dim)
    return shard


def activate(values):
    widened = values.astype(jnp.float32)
    scaled = widened * lax.rsqrt(jnp.mean(widened * widened, axis=-1, keepdims=True) + 1e-06)
    return jax.nn.silu(scaled).astype(jnp.bfloat16)


def double_size(values):
    return jnp.repeat(jnp.repeat(values, 2, axis=1), 2, axis=2)


def time_padded(values):
    return jnp.pad(values, ((2, 0), (0, 0), (0, 0), (0, 0)))


def stencil_columns(extended):
    padded = time_padded(extended)
    height = extended.shape[1] - 2
    breadth = extended.shape[2] - 2
    return jnp.concatenate(
        [
            padded[:, row_step : row_step + height, col_step : col_step + breadth, :]
            for row_step in range(3)
            for col_step in range(3)
        ],
        axis=-1,
    )


def apply_columns(columns, filters):
    frames = columns.shape[0] - 2
    folded = filters.reshape(3, 9 * filters.shape[3], filters.shape[4])
    total = jnp.dot(columns[0:frames], folded[0], preferred_element_type=jnp.float32)
    for frame_step in (1, 2):
        total = total + jnp.dot(
            columns[frame_step : frame_step + frames],
            folded[frame_step],
            preferred_element_type=jnp.float32,
        )
    return total


def coarse_conv(extended, filters):
    padded = time_padded(extended)
    frames = extended.shape[0]
    height = extended.shape[1] - 2
    breadth = extended.shape[2] - 2
    inputs = filters.shape[3]
    outputs = filters.shape[4]
    total = jnp.zeros((frames, height, breadth, outputs), jnp.float32)
    for frame_step in range(3):
        spread = jnp.transpose(filters[frame_step], (2, 0, 1, 3)).reshape(inputs, 9 * outputs)
        products = jnp.dot(
            padded[frame_step : frame_step + frames], spread, preferred_element_type=jnp.float32
        )
        for row_step in range(3):
            for col_step in range(3):
                lane = 3 * row_step + col_step
                total = (
                    total
                    + products[
                        :,
                        row_step : row_step + height,
                        col_step : col_step + breadth,
                        lane * outputs : (lane + 1) * outputs,
                    ]
                )
    return total


def middle_conv(extended, mid_filters):
    columns = stencil_columns(extended)
    return apply_columns(columns, lax.all_gather(mid_filters, "tile", axis=4, tiled=True))


def body(latent, coarse_filters, mid_filters, fine_filters, coarse_proj, mid_proj):
    first_act = activate(latent)
    whole = lax.all_gather(first_act, "grp", axis=1, tiled=True)
    widened = with_halo(whole, (("tile", 2),), 1)
    padded = jnp.pad(widened, ((0, 0), (1, 1), (0, 0), (0, 0)))
    filtered = coarse_conv(padded, coarse_filters).astype(jnp.bfloat16)
    returned = lax.all_to_all(filtered, "grp", split_axis=1, concat_axis=3, tiled=True)
    level_zero = (latent.astype(jnp.float32) + returned.astype(jnp.float32)).astype(jnp.bfloat16)
    reduced = jnp.dot(level_zero, coarse_proj, preferred_element_type=jnp.float32).astype(
        jnp.bfloat16
    )
    mid_act = double_size(activate(reduced))
    mid_ext = with_halo(mid_act, (("grp", 1), ("tile", 2)), 1)
    mid_terms = middle_conv(mid_ext, mid_filters)
    mid_out = (double_size(reduced).astype(jnp.float32) + mid_terms).astype(jnp.bfloat16)
    fine_low = jnp.dot(mid_out, mid_proj, preferred_element_type=jnp.float32).astype(jnp.bfloat16)
    fine_in = double_size(fine_low)
    fine_act = double_size(activate(fine_low))
    fine_ext = with_halo(fine_act, (("grp", 1), ("tile", 2)), 1)
    fine_terms = apply_columns(stencil_columns(fine_ext), fine_filters)
    return (fine_in.astype(jnp.float32) + fine_terms).astype(jnp.bfloat16)


def solution(mesh):
    in_specs = (
        P(None, "grp", "tile", None),
        P(None, None, None, None, "grp"),
        P(None, None, None, None, "tile"),
        P(),
        P(),
        P(),
    )
    out_specs = P(None, "grp", "tile", None)
    return jax.shard_map(body, mesh=mesh, in_specs=in_specs, out_specs=out_specs, check_vma=False)
```

profile of v0, /device:TPU:7, one launch (start us, length us, event | category | flops | bytes accessed | tf_op | source)
XLA Modules:
  0.0 200.4 jit_solution(11646952750403236550)
XLA Ops:
  10.0 61.1 %all-gather.3.cloned.1.call-done = bf16[8,64,2,512]{3,0,2,1:T(8,128)(2,1)} async-done(((bf16[8,4,2,512]{3,0,2,1:T(8,128)(2,1)}), bf16[8,64,2,512]{3,0,2,1:T(8,128)(2,1)}) %all-gather.3.cloned.1.call-update) | async-done | bytes 1048592 | tf_op jit(solution)/shard_map/all_gather | solution.py:96
  73.0 5.1 %collective-permute-start = (bf16[8,64,1,512]{3,1,2,0:T(8,128)(2,1)S(1)}, bf16[8,64,1,512]{3,1,2,0:T(8,128)(2,1)S(1)}, u32[]{:S(2)}, u32[]{:S(2)}) collective-permute-start(bf16[8,64,1,512]{3,1,2,0:T(8,128)(2,1)S(1)} %get-tuple-element.8), channel_id=1, source_target_pairs={{0,1},{1,2},{2,3},{3,4},{4,5},{5,6},{6,7},{7,8},{8,9},{9,10},{10,1... | collective-permute-start | bytes 1572872 | tf_op jit(solution)/shard_map/ppermute | solution.py:14
  80.0 4.1 %collective-permute-done = bf16[8,64,1,512]{3,1,2,0:T(8,128)(2,1)S(1)} collective-permute-done((bf16[8,64,1,512]{3,1,2,0:T(8,128)(2,1)S(1)}, bf16[8,64,1,512]{3,1,2,0:T(8,128)(2,1)S(1)}, u32[]{:S(2)}, u32[]{:S(2)}) %collective-permute-start) | collective-permute-done | bytes 524320 | tf_op jit(solution)/shard_map/ppermute | solution.py:14
  84.1 4.4 %collective-permute-done.1 = bf16[8,64,1,512]{3,1,2,0:T(8,128)(2,1)S(1)} collective-permute-done((bf16[8,64,1,512]{3,1,2,0:T(8,128)(2,1)S(1)}, bf16[8,64,1,512]{3,1,2,0:T(8,128)(2,1)S(1)}, u32[]{:S(2)}, u32[]{:S(2)}) %collective-permute-start.1) | collective-permute-done | bytes 524320 | tf_op jit(solution)/shard_map/ppermute | solution.py:15
  93.9 2.5 %fusion.24 = bf16[8,64,2,32]{3,1,2,0:T(8,128)(2,1)S(1)} fusion(f32[8,66,4,288]{3,1,2,0:T(8,128)S(1)} %fusion.47, f32[8,66,4,288]{3,1,2,0:T(8,128)S(1)} %fusion.51, f32[8,66,4,288]{3,1,2,0:T(8,128)S(1)} %fusion.50), kind=kLoop, calls=%fused_computation.35 | loop fusion | flops 884736 | bytes 3604480 | tf_op jit(solution)/shard_map/convert_element_type | solution.py:99
  97.0 9.8 %all_to_all.4 = bf16[16,2,1024]{2,1,0:T(2,128)(2,1)S(1)} all-to-all(bf16[16,2,1024]{2,1,0:T(2,128)(2,1)S(1)} %reshape.91), channel_id=1, replica_groups=mesh['grp'=16,'tile'=32] {'grp'}, dimensions={0} | all-to-all | bytes 131072 | tf_op jit(solution)/shard_map/all_to_all | solution.py:100
  108.0 3.7 %collective-permute-start.2 = (bf16[8,1,4,256]{3,2,1,0:T(4,128)(2,1)S(1)}, bf16[8,1,4,256]{3,2,1,0:T(4,128)(2,1)S(1)}, u32[]{:S(2)}, u32[]{:S(2)}) collective-permute-start(bf16[8,1,4,256]{3,2,1,0:T(4,128)(2,1)S(1)} %get-tuple-element.23), channel_id=1, source_target_pairs={{0,32},{32,64},{64,96},{96,128},{128,160},{160,192},{192,224},{224... | collective-permute-start | bytes 49160 | tf_op jit(solution)/shard_map/ppermute | solution.py:14
  111.7 1.9 collective-permute-start.3
  113.7 4.6 %collective-permute-done.3 = bf16[8,1,4,256]{3,2,1,0:T(4,128)(2,1)S(1)} collective-permute-done((bf16[8,1,4,256]{3,2,1,0:T(4,128)(2,1)S(1)}, bf16[8,1,4,256]{3,2,1,0:T(4,128)(2,1)S(1)}, u32[]{:S(2)}, u32[]{:S(2)}) %collective-permute-start.3) | collective-permute-done | bytes 16416 | tf_op jit(solution)/shard_map/ppermute | solution.py:15
  118.4 4.6 %collective-permute-start.4 = (bf16[8,10,1,256]{3,2,1,0:T(2,128)(2,1)S(1)}, bf16[8,10,1,256]{3,2,1,0:T(2,128)(2,1)S(1)}, u32[]{:S(2)}, u32[]{:S(2)}) collective-permute-start(bf16[8,10,1,256]{3,2,1,0:T(2,128)(2,1)S(1)} %get-tuple-element.20), channel_id=1, source_target_pairs={{0,1},{1,2},{2,3},{3,4},{4,5},{5,6},{6,7},{7,8},{8,9},{9,10},{10,1... | collective-permute-start | bytes 122888 | tf_op jit(solution)/shard_map/ppermute | solution.py:14
  123.1 2.1 %collective-permute-start.5 = (bf16[8,10,1,256]{3,2,1,0:T(2,128)(2,1)S(1)}, bf16[8,10,1,256]{3,2,1,0:T(2,128)(2,1)S(1)}, u32[]{:S(2)}, u32[]{:S(2)}) collective-permute-start(bf16[8,10,1,256]{3,2,1,0:T(2,128)(2,1)S(1)} %get-tuple-element.21), channel_id=1, source_target_pairs={{1,0},{2,1},{3,2},{4,3},{5,4},{6,5},{7,6},{8,7},{9,8},{10,9},{11,1... | collective-permute-start | bytes 122888 | tf_op jit(solution)/shard_map/ppermute | solution.py:15
  125.6 3.7 %collective-permute-done.5 = bf16[8,10,1,256]{3,2,1,0:T(2,128)(2,1)S(1)} collective-permute-done((bf16[8,10,1,256]{3,2,1,0:T(2,128)(2,1)S(1)}, bf16[8,10,1,256]{3,2,1,0:T(2,128)(2,1)S(1)}, u32[]{:S(2)}, u32[]{:S(2)}) %collective-permute-start.5) | collective-permute-done | bytes 40992 | tf_op jit(solution)/shard_map/ppermute | solution.py:15
  136.8 16.2 %all-gather.5.cloned.1.call-done = bf16[3,3,3,256,256]{3,4,2,1,0:T(8,128)(2,1)} async-done(((bf16[3,3,3,256,8]{3,4,2,1,0:T(8,128)(2,1)}), bf16[3,3,3,256,256]{3,4,2,1,0:T(8,128)(2,1)}) %all-gather.5.cloned.1.call-update) | async-done | bytes 3538960 | tf_op jit(solution)/shard_map/all_gather | solution.py:91
  153.0 3.3 %fusion.40 = (bf16[1,3,3,256,256]{3,4,2,1,0:T(8,128)(2,1)S(1)}, bf16[1,3,3,256,256]{3,4,2,1,0:T(8,128)(2,1)S(1)}, bf16[1,3,3,256,256]{3,4,2,1,0:T(8,128)(2,1)}) fusion(bf16[3,3,3,256,256]{3,4,2,1,0:T(8,128)(2,1)} %all-gather.5.cloned.1.call-done), kind=kLoop, calls=%fused_computation.110 | loop fusion | bytes 7077888 | tf_op jit(solution)/shard_map/slice | solution.py:55
  156.3 2.4 %copy.49 = bf16[1,3,3,256,256]{4,3,2,1,0:T(8,128)(2,1)} copy(bf16[1,3,3,256,256]{3,4,2,1,0:T(8,128)(2,1)} %get-tuple-element.7) | data formatting | bytes 2359296
  161.0 2.4 %fusion.48 = f32[8,8,4,256]{3,2,1,0:T(4,128)S(1)} fusion(bf16[10,8,4,2304]{3,2,1,0:T(4,128)(2,1)} %slice_dynamic-update-slice_fusion.9, bf16[2304,256,1,1]{1,0,3,2:T(8,128)(2,1)} %bitcast.115), kind=kOutput, calls=%fused_computation.119 | convolution fusion | flops 301989888 | bytes 2916352 | tf_op jit(solution)/shard_map/dot_general | solution.py:51
  163.4 2.0 convolution_add_fusion.3
  165.4 2.1 %fusion.14 = bf16[8,8,4,256]{3,2,1,0:T(4,128)(2,1)S(1)} fusion(f32[8,8,4,256]{3,2,1,0:T(4,128)S(1)} %convert_element_type.86, f32[8,8,4,256]{3,2,1,0:T(4,128)S(1)} %convolution_add_fusion.3, bf16[10,8,4,2304]{3,2,1,0:T(4,128)(2,1)} %slice_dynamic-update-slice_fusion.9, bf16[2304,256,1,1]{1,0,3,2:T(8,128)(2,1)S(1)} %bitcast.114), kind=kOutput, calls=%fused_computation.21 | convolution fusion | flops 302186496 | bytes 3309568 | tf_op jit(solution)/shard_map/dot_general | solution.py:53
  168.2 2.7 %collective-permute-start.6 = (bf16[8,1,8,128]{3,2,1,0:T(8,128)(2,1)S(1)}, bf16[8,1,8,128]{3,2,1,0:T(8,128)(2,1)S(1)}, u32[]{:S(2)}, u32[]{:S(2)}) collective-permute-start(bf16[8,1,8,128]{3,2,1,0:T(8,128)(2,1)S(1)} %get-tuple-element.18), channel_id=1, source_target_pairs={{0,32},{32,64},{64,96},{96,128},{128,160},{160,192},{192,224},{224... | collective-permute-start | bytes 49160 | tf_op jit(solution)/shard_map/ppermute | solution.py:14
  170.9 2.6 %collective-permute-start.7 = (bf16[8,1,8,128]{3,2,1,0:T(8,128)(2,1)S(1)}, bf16[8,1,8,128]{3,2,1,0:T(8,128)(2,1)S(1)}, u32[]{:S(2)}, u32[]{:S(2)}) collective-permute-start(bf16[8,1,8,128]{3,2,1,0:T(8,128)(2,1)S(1)} %get-tuple-element.19), channel_id=1, source_target_pairs={{32,0},{64,32},{96,64},{128,96},{160,128},{192,160},{224,192},{256... | collective-permute-start | bytes 49160 | tf_op jit(solution)/shard_map/ppermute | solution.py:15
  173.5 4.0 %collective-permute-done.7 = bf16[8,1,8,128]{3,2,1,0:T(8,128)(2,1)S(1)} collective-permute-done((bf16[8,1,8,128]{3,2,1,0:T(8,128)(2,1)S(1)}, bf16[8,1,8,128]{3,2,1,0:T(8,128)(2,1)S(1)}, u32[]{:S(2)}, u32[]{:S(2)}) %collective-permute-start.7) | collective-permute-done | bytes 16416 | tf_op jit(solution)/shard_map/ppermute | solution.py:15
  177.6 5.2 %collective-permute-start.8 = (bf16[8,18,1,128]{3,2,1,0:T(2,128)(2,1)S(1)}, bf16[8,18,1,128]{3,2,1,0:T(2,128)(2,1)S(1)}, u32[]{:S(2)}, u32[]{:S(2)}) collective-permute-start(bf16[8,18,1,128]{3,2,1,0:T(2,128)(2,1)S(1)} %get-tuple-element.16), channel_id=1, source_target_pairs={{0,1},{1,2},{2,3},{3,4},{4,5},{5,6},{6,7},{7,8},{8,9},{9,10},{10,1... | collective-permute-start | bytes 110600 | tf_op jit(solution)/shard_map/ppermute | solution.py:14
  182.9 1.9 collective-permute-start.9
  184.9 3.6 %collective-permute-done.9 = bf16[8,18,1,128]{3,2,1,0:T(2,128)(2,1)S(1)} collective-permute-done((bf16[8,18,1,128]{3,2,1,0:T(2,128)(2,1)S(1)}, bf16[8,18,1,128]{3,2,1,0:T(2,128)(2,1)S(1)}, u32[]{:S(2)}, u32[]{:S(2)}) %collective-permute-start.9) | collective-permute-done | bytes 36896 | tf_op jit(solution)/shard_map/ppermute | solution.py:15
  (89 shorter events, 30.5 us)
Async XLA Ops:
  6.5 100.8 %copy-start = (bf16[512,256]{1,0:T(8,128)(2,1)S(1)}, bf16[512,256]{1,0:T(8,128)(2,1)}, u32[]{:S(2)}) copy-start(bf16[512,256]{1,0:T(8,128)(2,1)} %param.10) | copy-start | bytes 786436
  6.5 73.4 %copy-start.2 = (bf16[3,3,3,512,32]{3,4,2,1,0:T(8,128)(2,1)S(1)}, bf16[3,3,3,512,32]{3,4,2,1,0:T(8,128)(2,1)}, u32[]{:S(2)}) copy-start(bf16[3,3,3,512,32]{3,4,2,1,0:T(8,128)(2,1)} %param.7) | copy-start | bytes 2654212
  6.5 64.5 %all-gather.3.cloned.1.call-start = ((), (), s32[]{:S(2)}) async-start(), calls=%async_computation.1 | async-start | bytes 1114112 | tf_op jit(solution)/shard_map/all_gather | solution.py:96
  9.2 143.8 %all-gather.5.cloned.1.call-start = ((), (), s32[]{:S(2)}) async-start(), calls=%async_computation.2 | async-start | bytes 3649536 | tf_op jit(solution)/shard_map/all_gather | solution.py:91
  73.0 11.2 %collective-permute-start = (bf16[8,64,1,512]{3,1,2,0:T(8,128)(2,1)S(1)}, bf16[8,64,1,512]{3,1,2,0:T(8,128)(2,1)S(1)}, u32[]{:S(2)}, u32[]{:S(2)}) collective-permute-start(bf16[8,64,1,512]{3,1,2,0:T(8,128)(2,1)S(1)} %get-tuple-element.8), channel_id=1, source_target_pairs={{0,1},{1,2},{2,3},{3,4},{4,5},{5,6},{6,7},{7,8},{8,9},{9,10},{10,1... | collective-permute-start | bytes 1572872 | tf_op jit(solution)/shard_map/ppermute | solution.py:14
  78.0 10.5 %collective-permute-start.1 = (bf16[8,64,1,512]{3,1,2,0:T(8,128)(2,1)S(1)}, bf16[8,64,1,512]{3,1,2,0:T(8,128)(2,1)S(1)}, u32[]{:S(2)}, u32[]{:S(2)}) collective-permute-start(bf16[8,64,1,512]{3,1,2,0:T(8,128)(2,1)S(1)} %get-tuple-element.9), channel_id=1, source_target_pairs={{1,0},{2,1},{3,2},{4,3},{5,4},{6,5},{7,6},{8,7},{9,8},{10,9},{11,1... | collective-permute-start | bytes 1572872 | tf_op jit(solution)/shard_map/ppermute | solution.py:15
  96.4 10.9 %copy-start.4 = (bf16[8,4,2,512]{3,2,1,0:T(2,128)(2,1)S(1)}, bf16[8,4,2,512]{3,2,1,0:T(2,128)(2,1)}, u32[]{:S(2)}) copy-start(bf16[8,4,2,512]{3,2,1,0:T(2,128)(2,1)} %param.6) | copy-start | bytes 196612
  108.0 5.6 %collective-permute-start.2 = (bf16[8,1,4,256]{3,2,1,0:T(4,128)(2,1)S(1)}, bf16[8,1,4,256]{3,2,1,0:T(4,128)(2,1)S(1)}, u32[]{:S(2)}, u32[]{:S(2)}) collective-permute-start(bf16[8,1,4,256]{3,2,1,0:T(4,128)(2,1)S(1)} %get-tuple-element.23), channel_id=1, source_target_pairs={{0,32},{32,64},{64,96},{96,128},{128,160},{160,192},{192,224},{224... | collective-permute-start | bytes 49160 | tf_op jit(solution)/shard_map/ppermute | solution.py:14
  111.7 6.6 %collective-permute-start.3 = (bf16[8,1,4,256]{3,2,1,0:T(4,128)(2,1)S(1)}, bf16[8,1,4,256]{3,2,1,0:T(4,128)(2,1)S(1)}, u32[]{:S(2)}, u32[]{:S(2)}) collective-permute-start(bf16[8,1,4,256]{3,2,1,0:T(4,128)(2,1)S(1)} %get-tuple-element.22), channel_id=1, source_target_pairs={{32,0},{64,32},{96,64},{128,96},{160,128},{192,160},{224,192},{256... | collective-permute-start | bytes 49160 | tf_op jit(solution)/shard_map/ppermute | solution.py:15
  118.4 7.2 %collective-permute-start.4 = (bf16[8,10,1,256]{3,2,1,0:T(2,128)(2,1)S(1)}, bf16[8,10,1,256]{3,2,1,0:T(2,128)(2,1)S(1)}, u32[]{:S(2)}, u32[]{:S(2)}) collective-permute-start(bf16[8,10,1,256]{3,2,1,0:T(2,128)(2,1)S(1)} %get-tuple-element.20), channel_id=1, source_target_pairs={{0,1},{1,2},{2,3},{3,4},{4,5},{5,6},{6,7},{7,8},{8,9},{9,10},{10,1... | collective-permute-start | bytes 122888 | tf_op jit(solution)/shard_map/ppermute | solution.py:14
  123.1 6.3 %collective-permute-start.5 = (bf16[8,10,1,256]{3,2,1,0:T(2,128)(2,1)S(1)}, bf16[8,10,1,256]{3,2,1,0:T(2,128)(2,1)S(1)}, u32[]{:S(2)}, u32[]{:S(2)}) collective-permute-start(bf16[8,10,1,256]{3,2,1,0:T(2,128)(2,1)S(1)} %get-tuple-element.21), channel_id=1, source_target_pairs={{1,0},{2,1},{3,2},{4,3},{5,4},{6,5},{7,6},{8,7},{9,8},{10,9},{11,1... | collective-permute-start | bytes 122888 | tf_op jit(solution)/shard_map/ppermute | solution.py:15
  161.0 2.4 %copy-start.1 = (bf16[1,3,3,256,256]{4,3,2,1,0:T(8,128)(2,1)S(1)}, bf16[1,3,3,256,256]{4,3,2,1,0:T(8,128)(2,1)}, u32[]{:S(2)}) copy-start(bf16[1,3,3,256,256]{4,3,2,1,0:T(8,128)(2,1)} %copy.50) | copy-start | bytes 3538948
  165.4 2.1 %copy-start.5 = (bf16[256,128]{1,0:T(8,128)(2,1)S(1)}, bf16[256,128]{1,0:T(8,128)(2,1)}, u32[]{:S(2)}) copy-start(bf16[256,128]{1,0:T(8,128)(2,1)} %param.11) | copy-start | bytes 196612
  165.4 19.4 %copy-start.3 = (bf16[3,3,3,128,128]{4,3,2,1,0:T(8,128)(2,1)S(1)}, bf16[3,3,3,128,128]{4,3,2,1,0:T(8,128)(2,1)}, u32[]{:S(2)}) copy-start(bf16[3,3,3,128,128]{4,3,2,1,0:T(8,128)(2,1)} %param.9) | copy-start | bytes 2654212
  168.2 5.3 %collective-permute-start.6 = (bf16[8,1,8,128]{3,2,1,0:T(8,128)(2,1)S(1)}, bf16[8,1,8,128]{3,2,1,0:T(8,128)(2,1)S(1)}, u32[]{:S(2)}, u32[]{:S(2)}) collective-permute-start(bf16[8,1,8,128]{3,2,1,0:T(8,128)(2,1)S(1)} %get-tuple-element.18), channel_id=1, source_target_pairs={{0,32},{32,64},{64,96},{96,128},{128,160},{160,192},{192,224},{224... | collective-permute-start | bytes 49160 | tf_op jit(solution)/shard_map/ppermute | solution.py:14
  170.9 6.6 %collective-permute-start.7 = (bf16[8,1,8,128]{3,2,1,0:T(8,128)(2,1)S(1)}, bf16[8,1,8,128]{3,2,1,0:T(8,128)(2,1)S(1)}, u32[]{:S(2)}, u32[]{:S(2)}) collective-permute-start(bf16[8,1,8,128]{3,2,1,0:T(8,128)(2,1)S(1)} %get-tuple-element.19), channel_id=1, source_target_pairs={{32,0},{64,32},{96,64},{128,96},{160,128},{192,160},{224,192},{256... | collective-permute-start | bytes 49160 | tf_op jit(solution)/shard_map/ppermute | solution.py:15
  177.6 7.3 %collective-permute-start.8 = (bf16[8,18,1,128]{3,2,1,0:T(2,128)(2,1)S(1)}, bf16[8,18,1,128]{3,2,1,0:T(2,128)(2,1)S(1)}, u32[]{:S(2)}, u32[]{:S(2)}) collective-permute-start(bf16[8,18,1,128]{3,2,1,0:T(2,128)(2,1)S(1)} %get-tuple-element.16), channel_id=1, source_target_pairs={{0,1},{1,2},{2,3},{3,4},{4,5},{5,6},{6,7},{7,8},{8,9},{9,10},{10,1... | collective-permute-start | bytes 110600 | tf_op jit(solution)/shard_map/ppermute | solution.py:14
  182.9 5.7 %collective-permute-start.9 = (bf16[8,18,1,128]{3,2,1,0:T(2,128)(2,1)S(1)}, bf16[8,18,1,128]{3,2,1,0:T(2,128)(2,1)S(1)}, u32[]{:S(2)}, u32[]{:S(2)}) collective-permute-start(bf16[8,18,1,128]{3,2,1,0:T(2,128)(2,1)S(1)} %get-tuple-element.17), channel_id=1, source_target_pairs={{1,0},{2,1},{3,2},{4,3},{5,4},{6,5},{7,6},{8,7},{9,8},{10,9},{11,1... | collective-permute-start | bytes 110600 | tf_op jit(solution)/shard_map/ppermute | solution.py:15
Sparse Core Ops, SparseCore 0:
  10.4 60.6 all-gather.2
  73.1 79.7 all-gather.4
where the time goes:
time: 201 us; the launch traced here: 200 us
  waiting for transfers between devices  102 us (51%)
  starting transfers between devices  31.8 us (16%)
  local copies, waits for them, and re-layouts  20.9 us (10%)
  matrix products  14.4 us (7%)
  between operations  13.9 us (7%)
  blocking collectives  9.77 us (5%)
  other arithmetic  7.18 us (4%)
    all_gather x1, waiting for transfers between devices, body(): whole = lax.all_gather(first_act, 'grp', axis=1, tiled=True)  61.1 us
    ppermute x5, starting transfers between devices, with_halo(): before = lax.ppermute(last, axis, up)  21.3 us
    ppermute x5, waiting for transfers between devices, with_halo(): after = lax.ppermute(initial, axis, down)  20.3 us
    all_gather x1, waiting for transfers between devices, middle_conv(): lax.all_gather(mid_filters, 'tile', axis=4, tiled=True)  16.2 us
    unnamed x35, local copies, waits for them, and re-layouts  12.7 us
    ppermute x5, starting transfers between devices, with_halo(): after = lax.ppermute(initial, axis, down)  10.5 us
    all_to_all x1, blocking collectives, body(): lax.all_to_all(filtered, 'grp', split_axis=1, concat_axis=3, tiled=True)  9.77 us
    dot_general x4, matrix products, apply_columns(): jnp.dot(columns[frame_step:frame_step + frames], folded[frame_step], pref...  6.33 us
  transfers between devices with their start and end apart: 12, of which 8 were waited for; matrix products, arithmetic and copies ran while one was open for 10% of the time, Pallas kernels for 0%

commit v1 on v0

--- a/solution.py
+++ b/solution.py
@@ -2,6 +2,22 @@
 import jax.numpy as jnp
 from jax import lax
 from jax.sharding import PartitionSpec as P
+
+
+def gather_around(x, axis, dim):
+    ways, here, turn = (lax.axis_size(axis), lax.axis_index(axis), x.shape[dim])
+    shape = [n * ways if d == dim else n for d, n in enumerate(x.shape)]
+    full = lax.dynamic_update_slice_in_dim(jnp.zeros(shape, x.dtype), x, here * turn, axis=dim)
+    going_up = going_down = x
+    for far in range(1, ways // 2 + 1):
+        going_up = lax.ppermute(going_up, axis, [(d, (d + 1) % ways) for d in range(ways)])
+        full = lax.dynamic_update_slice_in_dim(full, going_up, (here - far) % ways * turn, axis=dim)
+        if 2 * far < ways:
+            going_down = lax.ppermute(going_down, axis, [(d, (d - 1) % ways) for d in range(ways)])
+            full = lax.dynamic_update_slice_in_dim(
+                full, going_down, (here + far) % ways * turn, axis=dim
+            )
+    return full
 
 
 def with_halo(shard, sides, width):
@@ -93,7 +109,7 @@
 
 def body(latent, coarse_filters, mid_filters, fine_filters, coarse_proj, mid_proj):
     first_act = activate(latent)
-    whole = lax.all_gather(first_act, "grp", axis=1, tiled=True)
+    whole = gather_around(first_act, "grp", 1)
     widened = with_halo(whole, (("tile", 2),), 1)
     padded = jnp.pad(widened, ((0, 0), (1, 1), (0, 0), (0, 0)))
     filtered = coarse_conv(padded, coarse_filters).astype(jnp.bfloat16)

time: 201 us -> 195 us (0.970)
  the two profiles are of different devices: /device:TPU:7 before, /device:TPU:103 now
where the time goes in v1:
time: 195 us; the launch traced here: 194 us
  starting transfers between devices  90.2 us (46%)
  waiting for transfers between devices  29 us (15%)
  local copies, waits for them, and re-layouts  20.1 us (10%)
  blocking collectives  19.1 us (10%)
  between operations  14.6 us (7%)
  matrix products  14.4 us (7%)
  other arithmetic  6.59 us (3%)
    ppermute x8, starting transfers between devices, gather_around(): lax.ppermute(going_up, axis, [(d, (d + 1) % ways) for d in range(ways)])  41.3 us
    ppermute x5, starting transfers between devices, with_halo(): before = lax.ppermute(last, axis, up)  24 us
    ppermute x5, waiting for transfers between devices, with_halo(): after = lax.ppermute(initial, axis, down)  22.5 us
    all_to_all x1, blocking collectives, body(): lax.all_to_all(filtered, 'grp', split_axis=1, concat_axis=3, tiled=True)  19.1 us
    ppermute x7, starting transfers between devices, gather_around(): lax.ppermute(going_down, axis, [(d, (d - 1) % ways) for d in range(ways)])  13.7 us
    unnamed x35, local copies, waits for them, and re-layouts  12.6 us
    ppermute x5, starting transfers between devices, with_halo(): after = lax.ppermute(initial, axis, down)  11.2 us
    dot_general x4, matrix products, apply_columns(): jnp.dot(columns[frame_step:frame_step + frames], folded[frame_step], pref...  6.32 us
  transfers between devices with their start and end apart: 26, of which 7 were waited for; matrix products, arithmetic and copies ran while one was open for 10% of the time, Pallas kernels for 0%

profile of v1, /device:TPU:103, one launch (start us, length us, event | category | flops | bytes accessed | tf_op | source)
XLA Modules:
  0.0 193.9 jit_solution(14795854035309251484)
XLA Ops:
  8.9 3.3 %collective-permute-start = (bf16[8,4,2,512]{3,1,2,0:T(4,128)(2,1)S(1)}, bf16[8,4,2,512]{3,1,2,0:T(4,128)(2,1)S(1)}, u32[]{:S(2)}, u32[]{:S(2)}) collective-permute-start(bf16[8,4,2,512]{3,1,2,0:T(4,128)(2,1)S(1)} %get-tuple-element.6), channel_id=1, source_target_pairs={{0,32},{32,64},{64,96},{96,128},{128,160},{160,192},{192,224},{224... | collective-permute-start | bytes 196616 | tf_op jit(solution)/shard_map/ppermute | solution.py:13
  14.6 5.2 %collective-permute-start.2 = (bf16[8,4,2,512]{3,1,2,0:T(4,128)(2,1)S(1)}, bf16[8,4,2,512]{3,1,2,0:T(4,128)(2,1)S(1)}, u32[]{:S(2)}, u32[]{:S(2)}) collective-permute-start(bf16[8,4,2,512]{3,1,2,0:T(4,128)(2,1)S(1)} %collective-permute-done), channel_id=1, source_target_pairs={{0,32},{32,64},{64,96},{96,128},{128,160},{160,192},{192,224},{224... | collective-permute-start | bytes 196616 | tf_op jit(solution)/shard_map/ppermute | solution.py:13
  21.9 5.5 %collective-permute-start.4 = (bf16[8,4,2,512]{3,1,2,0:T(4,128)(2,1)S(1)}, bf16[8,4,2,512]{3,1,2,0:T(4,128)(2,1)S(1)}, u32[]{:S(2)}, u32[]{:S(2)}) collective-permute-start(bf16[8,4,2,512]{3,1,2,0:T(4,128)(2,1)S(1)} %collective-permute-done.2), channel_id=1, source_target_pairs={{0,32},{32,64},{64,96},{96,128},{128,160},{160,192},{192,224},{224... | collective-permute-start | bytes 196616 | tf_op jit(solution)/shard_map/ppermute | solution.py:13
  29.5 5.5 %collective-permute-start.6 = (bf16[8,4,2,512]{3,1,2,0:T(4,128)(2,1)S(1)}, bf16[8,4,2,512]{3,1,2,0:T(4,128)(2,1)S(1)}, u32[]{:S(2)}, u32[]{:S(2)}) collective-permute-start(bf16[8,4,2,512]{3,1,2,0:T(4,128)(2,1)S(1)} %collective-permute-done.4), channel_id=1, source_target_pairs={{0,32},{32,64},{64,96},{96,128},{128,160},{160,192},{192,224},{224... | collective-permute-start | bytes 196616 | tf_op jit(solution)/shard_map/ppermute | solution.py:13
  37.0 5.5 %collective-permute-start.8 = (bf16[8,4,2,512]{3,1,2,0:T(4,128)(2,1)S(1)}, bf16[8,4,2,512]{3,1,2,0:T(4,128)(2,1)S(1)}, u32[]{:S(2)}, u32[]{:S(2)}) collective-permute-start(bf16[8,4,2,512]{3,1,2,0:T(4,128)(2,1)S(1)} %collective-permute-done.6), channel_id=1, source_target_pairs={{0,32},{32,64},{64,96},{96,128},{128,160},{160,192},{192,224},{224... | collective-permute-start | bytes 196616 | tf_op jit(solution)/shard_map/ppermute | solution.py:13
  44.6 5.5 %collective-permute-start.10 = (bf16[8,4,2,512]{3,1,2,0:T(4,128)(2,1)S(1)}, bf16[8,4,2,512]{3,1,2,0:T(4,128)(2,1)S(1)}, u32[]{:S(2)}, u32[]{:S(2)}) collective-permute-start(bf16[8,4,2,512]{3,1,2,0:T(4,128)(2,1)S(1)} %collective-permute-done.8), channel_id=1, source_target_pairs={{0,32},{32,64},{64,96},{96,128},{128,160},{160,192},{192,224},{224... | collective-permute-start | bytes 196616 | tf_op jit(solution)/shard_map/ppermute | solution.py:13
  52.1 5.5 %collective-permute-start.12 = (bf16[8,4,2,512]{3,1,2,0:T(4,128)(2,1)S(1)}, bf16[8,4,2,512]{3,1,2,0:T(4,128)(2,1)S(1)}, u32[]{:S(2)}, u32[]{:S(2)}) collective-permute-start(bf16[8,4,2,512]{3,1,2,0:T(4,128)(2,1)S(1)} %collective-permute-done.10), channel_id=1, source_target_pairs={{0,32},{32,64},{64,96},{96,128},{128,160},{160,192},{192,224},{224... | collective-permute-start | bytes 196616 | tf_op jit(solution)/shard_map/ppermute | solution.py:13
  59.7 5.5 %collective-permute-start.14 = (bf16[8,4,2,512]{3,1,2,0:T(4,128)(2,1)S(1)}, bf16[8,4,2,512]{3,1,2,0:T(4,128)(2,1)S(1)}, u32[]{:S(2)}, u32[]{:S(2)}) collective-permute-start(bf16[8,4,2,512]{3,1,2,0:T(4,128)(2,1)S(1)} %collective-permute-done.12), channel_id=1, source_target_pairs={{0,32},{32,64},{64,96},{96,128},{128,160},{160,192},{192,224},{224... | collective-permute-start | bytes 196616 | tf_op jit(solution)/shard_map/ppermute | solution.py:13
  66.6 11.0 %collective-permute-start.15 = (bf16[8,64,1,512]{3,1,2,0:T(8,128)(2,1)S(1)}, bf16[8,64,1,512]{3,1,2,0:T(8,128)(2,1)S(1)}, u32[]{:S(2)}, u32[]{:S(2)}) collective-permute-start(bf16[8,64,1,512]{3,1,2,0:T(8,128)(2,1)S(1)} %get-tuple-element.10), channel_id=1, source_target_pairs={{0,1},{1,2},{2,3},{3,4},{4,5},{5,6},{6,7},{7,8},{8,9},{9,10},{10,1... | collective-permute-start | bytes 1572872 | tf_op jit(solution)/shard_map/ppermute | solution.py:30
  79.6 5.3 %collective-permute-done.15 = bf16[8,64,1,512]{3,1,2,0:T(8,128)(2,1)S(1)} collective-permute-done((bf16[8,64,1,512]{3,1,2,0:T(8,128)(2,1)S(1)}, bf16[8,64,1,512]{3,1,2,0:T(8,128)(2,1)S(1)}, u32[]{:S(2)}, u32[]{:S(2)}) %collective-permute-start.15) | collective-permute-done | bytes 524320 | tf_op jit(solution)/shard_map/ppermute | solution.py:30
  84.9 5.5 %collective-permute-done.16 = bf16[8,64,1,512]{3,1,2,0:T(8,128)(2,1)S(1)} collective-permute-done((bf16[8,64,1,512]{3,1,2,0:T(8,128)(2,1)S(1)}, bf16[8,64,1,512]{3,1,2,0:T(8,128)(2,1)S(1)}, u32[]{:S(2)}, u32[]{:S(2)}) %collective-permute-start.16) | collective-permute-done | bytes 524320 | tf_op jit(solution)/shard_map/ppermute | solution.py:31
  95.7 2.5 %fusion.24 = bf16[8,64,2,32]{3,1,2,0:T(8,128)(2,1)S(1)} fusion(f32[8,66,4,288]{3,1,2,0:T(8,128)S(1)} %fusion.48, f32[8,66,4,288]{3,1,2,0:T(8,128)S(1)} %fusion.52, f32[8,66,4,288]{3,1,2,0:T(8,128)S(1)} %fusion.51), kind=kLoop, calls=%fused_computation.35 | loop fusion | flops 884736 | bytes 3604480 | tf_op jit(solution)/shard_map/convert_element_type | solution.py:115
  98.8 19.1 %all_to_all.4 = bf16[16,2,1024]{2,1,0:T(2,128)(2,1)S(1)} all-to-all(bf16[16,2,1024]{2,1,0:T(2,128)(2,1)S(1)} %reshape.91), channel_id=1, replica_groups=mesh['grp'=16,'tile'=32] {'grp'}, dimensions={0} | all-to-all | bytes 131072 | tf_op jit(solution)/shard_map/all_to_all | solution.py:116
  119.2 3.7 %collective-permute-start.17 = (bf16[8,1,4,256]{3,2,1,0:T(4,128)(2,1)S(1)}, bf16[8,1,4,256]{3,2,1,0:T(4,128)(2,1)S(1)}, u32[]{:S(2)}, u32[]{:S(2)}) collective-permute-start(bf16[8,1,4,256]{3,2,1,0:T(4,128)(2,1)S(1)} %get-tuple-element.25), channel_id=1, source_target_pairs={{0,32},{32,64},{64,96},{96,128},{128,160},{160,192},{192,224},{224... | collective-permute-start | bytes 49160 | tf_op jit(solution)/shard_map/ppermute | solution.py:30
  125.1 4.4 %collective-permute-done.18 = bf16[8,1,4,256]{3,2,1,0:T(4,128)(2,1)S(1)} collective-permute-done((bf16[8,1,4,256]{3,2,1,0:T(4,128)(2,1)S(1)}, bf16[8,1,4,256]{3,2,1,0:T(4,128)(2,1)S(1)}, u32[]{:S(2)}, u32[]{:S(2)}) %collective-permute-start.18) | collective-permute-done | bytes 16416 | tf_op jit(solution)/shard_map/ppermute | solution.py:31
  129.6 4.4 %collective-permute-start.19 = (bf16[8,10,1,256]{3,2,1,0:T(2,128)(2,1)S(1)}, bf16[8,10,1,256]{3,2,1,0:T(2,128)(2,1)S(1)}, u32[]{:S(2)}, u32[]{:S(2)}) collective-permute-start(bf16[8,10,1,256]{3,2,1,0:T(2,128)(2,1)S(1)} %get-tuple-element.22), channel_id=1, source_target_pairs={{0,1},{1,2},{2,3},{3,4},{4,5},{5,6},{6,7},{7,8},{8,9},{9,10},{10,1... | collective-permute-start | bytes 122888 | tf_op jit(solution)/shard_map/ppermute | solution.py:30
  136.4 4.6 %collective-permute-done.20 = bf16[8,10,1,256]{3,2,1,0:T(2,128)(2,1)S(1)} collective-permute-done((bf16[8,10,1,256]{3,2,1,0:T(2,128)(2,1)S(1)}, bf16[8,10,1,256]{3,2,1,0:T(2,128)(2,1)S(1)}, u32[]{:S(2)}, u32[]{:S(2)}) %collective-permute-start.20) | collective-permute-done | bytes 40992 | tf_op jit(solution)/shard_map/ppermute | solution.py:31
  148.4 3.3 %fusion.41 = (bf16[1,3,3,256,256]{3,4,2,1,0:T(8,128)(2,1)S(1)}, bf16[1,3,3,256,256]{3,4,2,1,0:T(8,128)(2,1)S(1)}, bf16[1,3,3,256,256]{3,4,2,1,0:T(8,128)(2,1)}) fusion(bf16[3,3,3,256,256]{3,4,2,1,0:T(8,128)(2,1)} %all-gather.2.cloned.1.call-done), kind=kLoop, calls=%fused_computation.127 | loop fusion | bytes 7077888 | tf_op jit(solution)/shard_map/slice | solution.py:71
  151.7 2.4 %copy.78 = bf16[1,3,3,256,256]{4,3,2,1,0:T(8,128)(2,1)} copy(bf16[1,3,3,256,256]{3,4,2,1,0:T(8,128)(2,1)} %get-tuple-element.9) | data formatting | bytes 2359296
  156.3 2.4 %fusion.49 = f32[8,8,4,256]{3,2,1,0:T(4,128)S(1)} fusion(bf16[10,8,4,2304]{3,2,1,0:T(4,128)(2,1)} %slice_dynamic-update-slice_fusion.9, bf16[2304,256,1,1]{1,0,3,2:T(8,128)(2,1)} %bitcast.115), kind=kOutput, calls=%fused_computation.136 | convolution fusion | flops 301989888 | bytes 2916352 | tf_op jit(solution)/shard_map/dot_general | solution.py:67
  165.5 3.4 %collective-permute-start.22 = (bf16[8,1,8,128]{3,2,1,0:T(8,128)(2,1)S(1)}, bf16[8,1,8,128]{3,2,1,0:T(8,128)(2,1)S(1)}, u32[]{:S(2)}, u32[]{:S(2)}) collective-permute-start(bf16[8,1,8,128]{3,2,1,0:T(8,128)(2,1)S(1)} %get-tuple-element.21), channel_id=1, source_target_pairs={{32,0},{64,32},{96,64},{128,96},{160,128},{192,160},{224,192},{256... | collective-permute-start | bytes 49160 | tf_op jit(solution)/shard_map/ppermute | solution.py:31
  168.9 3.2 %collective-permute-done.22 = bf16[8,1,8,128]{3,2,1,0:T(8,128)(2,1)S(1)} collective-permute-done((bf16[8,1,8,128]{3,2,1,0:T(8,128)(2,1)S(1)}, bf16[8,1,8,128]{3,2,1,0:T(8,128)(2,1)S(1)}, u32[]{:S(2)}, u32[]{:S(2)}) %collective-permute-start.22) | collective-permute-done | bytes 16416 | tf_op jit(solution)/shard_map/ppermute | solution.py:31
  172.2 3.0 %collective-permute-start.23 = (bf16[8,18,1,128]{3,2,1,0:T(2,128)(2,1)S(1)}, bf16[8,18,1,128]{3,2,1,0:T(2,128)(2,1)S(1)}, u32[]{:S(2)}, u32[]{:S(2)}) collective-permute-start(bf16[8,18,1,128]{3,2,1,0:T(2,128)(2,1)S(1)} %get-tuple-element.18), channel_id=1, source_target_pairs={{0,1},{1,2},{2,3},{3,4},{4,5},{5,6},{6,7},{7,8},{8,9},{9,10},{10,1... | collective-permute-start | bytes 110600 | tf_op jit(solution)/shard_map/ppermute | solution.py:30
  177.3 4.8 %collective-permute-done.24 = bf16[8,18,1,128]{3,2,1,0:T(2,128)(2,1)S(1)} collective-permute-done((bf16[8,18,1,128]{3,2,1,0:T(2,128)(2,1)S(1)}, bf16[8,18,1,128]{3,2,1,0:T(2,128)(2,1)S(1)}, u32[]{:S(2)}, u32[]{:S(2)}) %collective-permute-start.24) | collective-permute-done | bytes 36896 | tf_op jit(solution)/shard_map/ppermute | solution.py:31
  (135 shorter events, 55.1 us)
Async XLA Ops:
  6.5 141.8 %all-gather.2.cloned.1.call-start = ((), (), s32[]{:S(2)}) async-start(), calls=%async_computation.1 | async-start | bytes 3649536 | tf_op jit(solution)/shard_map/all_gather | solution.py:107
  8.9 5.7 %collective-permute-start = (bf16[8,4,2,512]{3,1,2,0:T(4,128)(2,1)S(1)}, bf16[8,4,2,512]{3,1,2,0:T(4,128)(2,1)S(1)}, u32[]{:S(2)}, u32[]{:S(2)}) collective-permute-start(bf16[8,4,2,512]{3,1,2,0:T(4,128)(2,1)S(1)} %get-tuple-element.6), channel_id=1, source_target_pairs={{0,32},{32,64},{64,96},{96,128},{128,160},{160,192},{192,224},{224... | collective-permute-start | bytes 196616 | tf_op jit(solution)/shard_map/ppermute | solution.py:13
  12.2 7.7 %collective-permute-start.1 = (bf16[8,4,2,512]{3,1,2,0:T(4,128)(2,1)S(1)}, bf16[8,4,2,512]{3,1,2,0:T(4,128)(2,1)S(1)}, u32[]{:S(2)}, u32[]{:S(2)}) collective-permute-start(bf16[8,4,2,512]{3,1,2,0:T(4,128)(2,1)S(1)} %get-tuple-element.6), channel_id=1, source_target_pairs={{0,480},{32,0},{64,32},{96,64},{128,96},{160,128},{192,160},{224,1... | collective-permute-start | bytes 196616 | tf_op jit(solution)/shard_map/ppermute | solution.py:16
  14.6 7.3 %collective-permute-start.2 = (bf16[8,4,2,512]{3,1,2,0:T(4,128)(2,1)S(1)}, bf16[8,4,2,512]{3,1,2,0:T(4,128)(2,1)S(1)}, u32[]{:S(2)}, u32[]{:S(2)}) collective-permute-start(bf16[8,4,2,512]{3,1,2,0:T(4,128)(2,1)S(1)} %collective-permute-done), channel_id=1, source_target_pairs={{0,32},{32,64},{64,96},{96,128},{128,160},{160,192},{192,224},{224... | collective-permute-start | bytes 196616 | tf_op jit(solution)/shard_map/ppermute | solution.py:13
  19.9 7.5 %collective-permute-start.3 = (bf16[8,4,2,512]{3,1,2,0:T(4,128)(2,1)S(1)}, bf16[8,4,2,512]{3,1,2,0:T(4,128)(2,1)S(1)}, u32[]{:S(2)}, u32[]{:S(2)}) collective-permute-start(bf16[8,4,2,512]{3,1,2,0:T(4,128)(2,1)S(1)} %collective-permute-done.1), channel_id=1, source_target_pairs={{0,480},{32,0},{64,32},{96,64},{128,96},{160,128},{192,160},{224,1... | collective-permute-start | bytes 196616 | tf_op jit(solution)/shard_map/ppermute | solution.py:16
  21.9 7.5 %collective-permute-start.4 = (bf16[8,4,2,512]{3,1,2,0:T(4,128)(2,1)S(1)}, bf16[8,4,2,512]{3,1,2,0:T(4,128)(2,1)S(1)}, u32[]{:S(2)}, u32[]{:S(2)}) collective-permute-start(bf16[8,4,2,512]{3,1,2,0:T(4,128)(2,1)S(1)} %collective-permute-done.2), channel_id=1, source_target_pairs={{0,32},{32,64},{64,96},{96,128},{128,160},{160,192},{192,224},{224... | collective-permute-start | bytes 196616 | tf_op jit(solution)/shard_map/ppermute | solution.py:13
  27.4 7.5 %collective-permute-start.5 = (bf16[8,4,2,512]{3,1,2,0:T(4,128)(2,1)S(1)}, bf16[8,4,2,512]{3,1,2,0:T(4,128)(2,1)S(1)}, u32[]{:S(2)}, u32[]{:S(2)}) collective-permute-start(bf16[8,4,2,512]{3,1,2,0:T(4,128)(2,1)S(1)} %collective-permute-done.3), channel_id=1, source_target_pairs={{0,480},{32,0},{64,32},{96,64},{128,96},{160,128},{192,160},{224,1... | collective-permute-start | bytes 196616 | tf_op jit(solution)/shard_map/ppermute | solution.py:16
  29.5 7.5 %collective-permute-start.6 = (bf16[8,4,2,512]{3,1,2,0:T(4,128)(2,1)S(1)}, bf16[8,4,2,512]{3,1,2,0:T(4,128)(2,1)S(1)}, u32[]{:S(2)}, u32[]{:S(2)}) collective-permute-start(bf16[8,4,2,512]{3,1,2,0:T(4,128)(2,1)S(1)} %collective-permute-done.4), channel_id=1, source_target_pairs={{0,32},{32,64},{64,96},{96,128},{128,160},{160,192},{192,224},{224... | collective-permute-start | bytes 196616 | tf_op jit(solution)/shard_map/ppermute | solution.py:13
  35.0 7.5 %collective-permute-start.7 = (bf16[8,4,2,512]{3,1,2,0:T(4,128)(2,1)S(1)}, bf16[8,4,2,512]{3,1,2,0:T(4,128)(2,1)S(1)}, u32[]{:S(2)}, u32[]{:S(2)}) collective-permute-start(bf16[8,4,2,512]{3,1,2,0:T(4,128)(2,1)S(1)} %collective-permute-done.5), channel_id=1, source_target_pairs={{0,480},{32,0},{64,32},{96,64},{128,96},{160,128},{192,160},{224,1... | collective-permute-start | bytes 196616 | tf_op jit(solution)/shard_map/ppermute | solution.py:16
  37.0 7.5 %collective-permute-start.8 = (bf16[8,4,2,512]{3,1,2,0:T(4,128)(2,1)S(1)}, bf16[8,4,2,512]{3,1,2,0:T(4,128)(2,1)S(1)}, u32[]{:S(2)}, u32[]{:S(2)}) collective-permute-start(bf16[8,4,2,512]{3,1,2,0:T(4,128)(2,1)S(1)} %collective-permute-done.6), channel_id=1, source_target_pairs={{0,32},{32,64},{64,96},{96,128},{128,160},{160,192},{192,224},{224... | collective-permute-start | bytes 196616 | tf_op jit(solution)/shard_map/ppermute | solution.py:13
  42.5 7.5 %collective-permute-start.9 = (bf16[8,4,2,512]{3,1,2,0:T(4,128)(2,1)S(1)}, bf16[8,4,2,512]{3,1,2,0:T(4,128)(2,1)S(1)}, u32[]{:S(2)}, u32[]{:S(2)}) collective-permute-start(bf16[8,4,2,512]{3,1,2,0:T(4,128)(2,1)S(1)} %collective-permute-done.7), channel_id=1, source_target_pairs={{0,480},{32,0},{64,32},{96,64},{128,96},{160,128},{192,160},{224,1... | collective-permute-start | bytes 196616 | tf_op jit(solution)/shard_map/ppermute | solution.py:16
  44.6 7.5 %collective-permute-start.10 = (bf16[8,4,2,512]{3,1,2,0:T(4,128)(2,1)S(1)}, bf16[8,4,2,512]{3,1,2,0:T(4,128)(2,1)S(1)}, u32[]{:S(2)}, u32[]{:S(2)}) collective-permute-start(bf16[8,4,2,512]{3,1,2,0:T(4,128)(2,1)S(1)} %collective-permute-done.8), channel_id=1, source_target_pairs={{0,32},{32,64},{64,96},{96,128},{128,160},{160,192},{192,224},{224... | collective-permute-start | bytes 196616 | tf_op jit(solution)/shard_map/ppermute | solution.py:13
  50.1 7.5 %collective-permute-start.11 = (bf16[8,4,2,512]{3,1,2,0:T(4,128)(2,1)S(1)}, bf16[8,4,2,512]{3,1,2,0:T(4,128)(2,1)S(1)}, u32[]{:S(2)}, u32[]{:S(2)}) collective-permute-start(bf16[8,4,2,512]{3,1,2,0:T(4,128)(2,1)S(1)} %collective-permute-done.9), channel_id=1, source_target_pairs={{0,480},{32,0},{64,32},{96,64},{128,96},{160,128},{192,160},{224,1... | collective-permute-start | bytes 196616 | tf_op jit(solution)/shard_map/ppermute | solution.py:16
  52.1 7.5 %collective-permute-start.12 = (bf16[8,4,2,512]{3,1,2,0:T(4,128)(2,1)S(1)}, bf16[8,4,2,512]{3,1,2,0:T(4,128)(2,1)S(1)}, u32[]{:S(2)}, u32[]{:S(2)}) collective-permute-start(bf16[8,4,2,512]{3,1,2,0:T(4,128)(2,1)S(1)} %collective-permute-done.10), channel_id=1, source_target_pairs={{0,32},{32,64},{64,96},{96,128},{128,160},{160,192},{192,224},{224... | collective-permute-start | bytes 196616 | tf_op jit(solution)/shard_map/ppermute | solution.py:13
  57.6 7.6 %collective-permute-start.13 = (bf16[8,4,2,512]{3,1,2,0:T(4,128)(2,1)S(1)}, bf16[8,4,2,512]{3,1,2,0:T(4,128)(2,1)S(1)}, u32[]{:S(2)}, u32[]{:S(2)}) collective-permute-start(bf16[8,4,2,512]{3,1,2,0:T(4,128)(2,1)S(1)} %collective-permute-done.11), channel_id=1, source_target_pairs={{0,480},{32,0},{64,32},{96,64},{128,96},{160,128},{192,160},{224,1... | collective-permute-start | bytes 196616 | tf_op jit(solution)/shard_map/ppermute | solution.py:16
  59.7 6.8 %collective-permute-start.14 = (bf16[8,4,2,512]{3,1,2,0:T(4,128)(2,1)S(1)}, bf16[8,4,2,512]{3,1,2,0:T(4,128)(2,1)S(1)}, u32[]{:S(2)}, u32[]{:S(2)}) collective-permute-start(bf16[8,4,2,512]{3,1,2,0:T(4,128)(2,1)S(1)} %collective-permute-done.12), channel_id=1, source_target_pairs={{0,32},{32,64},{64,96},{96,128},{128,160},{160,192},{192,224},{224... | collective-permute-start | bytes 196616 | tf_op jit(solution)/shard_map/ppermute | solution.py:13
  66.6 18.3 %collective-permute-start.15 = (bf16[8,64,1,512]{3,1,2,0:T(8,128)(2,1)S(1)}, bf16[8,64,1,512]{3,1,2,0:T(8,128)(2,1)S(1)}, u32[]{:S(2)}, u32[]{:S(2)}) collective-permute-start(bf16[8,64,1,512]{3,1,2,0:T(8,128)(2,1)S(1)} %get-tuple-element.10), channel_id=1, source_target_pairs={{0,1},{1,2},{2,3},{3,4},{4,5},{5,6},{6,7},{7,8},{8,9},{9,10},{10,1... | collective-permute-start | bytes 1572872 | tf_op jit(solution)/shard_map/ppermute | solution.py:30
  77.6 12.8 %collective-permute-start.16 = (bf16[8,64,1,512]{3,1,2,0:T(8,128)(2,1)S(1)}, bf16[8,64,1,512]{3,1,2,0:T(8,128)(2,1)S(1)}, u32[]{:S(2)}, u32[]{:S(2)}) collective-permute-start(bf16[8,64,1,512]{3,1,2,0:T(8,128)(2,1)S(1)} %get-tuple-element.11), channel_id=1, source_target_pairs={{1,0},{2,1},{3,2},{4,3},{5,4},{6,5},{7,6},{8,7},{9,8},{10,9},{11,1... | collective-permute-start | bytes 1572872 | tf_op jit(solution)/shard_map/ppermute | solution.py:31
  119.2 5.8 %collective-permute-start.17 = (bf16[8,1,4,256]{3,2,1,0:T(4,128)(2,1)S(1)}, bf16[8,1,4,256]{3,2,1,0:T(4,128)(2,1)S(1)}, u32[]{:S(2)}, u32[]{:S(2)}) collective-permute-start(bf16[8,1,4,256]{3,2,1,0:T(4,128)(2,1)S(1)} %get-tuple-element.25), channel_id=1, source_target_pairs={{0,32},{32,64},{64,96},{96,128},{128,160},{160,192},{192,224},{224... | collective-permute-start | bytes 49160 | tf_op jit(solution)/shard_map/ppermute | solution.py:30
  122.9 6.6 %collective-permute-start.18 = (bf16[8,1,4,256]{3,2,1,0:T(4,128)(2,1)S(1)}, bf16[8,1,4,256]{3,2,1,0:T(4,128)(2,1)S(1)}, u32[]{:S(2)}, u32[]{:S(2)}) collective-permute-start(bf16[8,1,4,256]{3,2,1,0:T(4,128)(2,1)S(1)} %get-tuple-element.24), channel_id=1, source_target_pairs={{32,0},{64,32},{96,64},{128,96},{160,128},{192,160},{224,192},{256... | collective-permute-start | bytes 49160 | tf_op jit(solution)/shard_map/ppermute | solution.py:31
  129.6 6.8 %collective-permute-start.19 = (bf16[8,10,1,256]{3,2,1,0:T(2,128)(2,1)S(1)}, bf16[8,10,1,256]{3,2,1,0:T(2,128)(2,1)S(1)}, u32[]{:S(2)}, u32[]{:S(2)}) collective-permute-start(bf16[8,10,1,256]{3,2,1,0:T(2,128)(2,1)S(1)} %get-tuple-element.22), channel_id=1, source_target_pairs={{0,1},{1,2},{2,3},{3,4},{4,5},{5,6},{6,7},{7,8},{8,9},{9,10},{10,1... | collective-permute-start | bytes 122888 | tf_op jit(solution)/shard_map/ppermute | solution.py:30
  134.1 7.0 %collective-permute-start.20 = (bf16[8,10,1,256]{3,2,1,0:T(2,128)(2,1)S(1)}, bf16[8,10,1,256]{3,2,1,0:T(2,128)(2,1)S(1)}, u32[]{:S(2)}, u32[]{:S(2)}) collective-permute-start(bf16[8,10,1,256]{3,2,1,0:T(2,128)(2,1)S(1)} %get-tuple-element.23), channel_id=1, source_target_pairs={{1,0},{2,1},{3,2},{4,3},{5,4},{6,5},{7,6},{8,7},{9,8},{10,9},{11,1... | collective-permute-start | bytes 122888 | tf_op jit(solution)/shard_map/ppermute | solution.py:31
  165.5 6.6 %collective-permute-start.22 = (bf16[8,1,8,128]{3,2,1,0:T(8,128)(2,1)S(1)}, bf16[8,1,8,128]{3,2,1,0:T(8,128)(2,1)S(1)}, u32[]{:S(2)}, u32[]{:S(2)}) collective-permute-start(bf16[8,1,8,128]{3,2,1,0:T(8,128)(2,1)S(1)} %get-tuple-element.21), channel_id=1, source_target_pairs={{32,0},{64,32},{96,64},{128,96},{160,128},{192,160},{224,192},{256... | collective-permute-start | bytes 49160 | tf_op jit(solution)/shard_map/ppermute | solution.py:31
  175.2 6.9 %collective-permute-start.24 = (bf16[8,18,1,128]{3,2,1,0:T(2,128)(2,1)S(1)}, bf16[8,18,1,128]{3,2,1,0:T(2,128)(2,1)S(1)}, u32[]{:S(2)}, u32[]{:S(2)}) collective-permute-start(bf16[8,18,1,128]{3,2,1,0:T(2,128)(2,1)S(1)} %get-tuple-element.19), channel_id=1, source_target_pairs={{1,0},{2,1},{3,2},{4,3},{5,4},{6,5},{7,6},{8,7},{9,8},{10,9},{11,1... | collective-permute-start | bytes 110600 | tf_op jit(solution)/shard_map/ppermute | solution.py:31
  (8 other events, 234.2 us)
Sparse Core Ops, SparseCore 0:
  14.5 82.7 all-gather.1
